TPU v7x, 512 devices: a whole 4x4x16 slice. The times are simulated.
512 devices in a mesh: snd: 32 (over y, x, core), rcv: 16 (over z).
Axes of the slice: x: 4, y: 4, z: 16, core: 2. Of those that a mesh axis runs over, the one named last changes fastest.
Arguments:
- nodes: bfloat16 [4096, 512], P(('snd', 'rcv')), may hold values from -6 to 6
- edges: bfloat16 [32, 16, 256, 512], P('snd', 'rcv'), may hold values from -6 to 6
- send_local: int32 [32, 16, 256], P('snd', 'rcv'), may hold values from 0 to 127
- recv_local: int32 [32, 16, 256], P('snd', 'rcv'), may hold values from 0 to 255
- edge_count: int32 [32, 16], P('snd', 'rcv'), may hold values from 32 to 256, as said below
- edge_w1: bfloat16 [1536, 512], replicated, may hold values from -0.15625 to 0.15625
- edge_w2: bfloat16 [512, 512], replicated, may hold values from -0.25 to 0.25
- node_w1: bfloat16 [1024, 512], replicated, may hold values from -0.1875 to 0.1875
- node_w2: bfloat16 [512, 512], replicated, may hold values from -0.25 to 0.25
- grad_nodes_out: bfloat16 [4096, 512], P(('snd', 'rcv')), may hold values from -6 to 6
- grad_edges_out: bfloat16 [32, 16, 256, 512], P('snd', 'rcv'), may hold values from -6 to 6
Outputs:
- grad_nodes: float32 [4096, 512], P(('snd', 'rcv'))
- grad_edges: float32 [32, 16, 256, 512], P('snd', 'rcv')
Inputs may be any that keep to these rules, and one draw needn't show every extreme that they name: Live edges of a tile fill its first edge_count slots; in every draw some tile has all 256 slots live.
All inputs are finite; a program needn't handle non-finite values.
Results may differ from a plain program's by a relative error of at most 0.019.
Values may be sent and summed in bfloat16 or wider, within the bound.
A program may use at most 64 MiB of HBM per device.

v0:
```python
import jax
import jax.numpy as jnp
from jax import lax
from jax.sharding import PartitionSpec as P


def swish_slope(pre_act):
    sigma = jax.nn.sigmoid(pre_act)
    return sigma * (1.0 + pre_act * (1.0 - sigma))


def layer_norm(values):
    center = values - jnp.mean(values, -1, keepdims=True)
    inv_scale = lax.rsqrt(jnp.mean(center * center, -1, keepdims=True) + 1e-05)
    return (center * inv_scale, inv_scale)


def norm_backward(upstream, normed, inv_scale):
    return inv_scale * (
        upstream
        - jnp.mean(upstream, -1, keepdims=True)
        - normed * jnp.mean(upstream * normed, -1, keepdims=True)
    )


def mlp_forward(inputs_cat, first_w, second_w):
    pre_act = jnp.dot(inputs_cat, first_w, preferred_element_type=jnp.float32)
    hidden = jax.nn.silu(pre_act).astype(jnp.bfloat16)
    output = jnp.dot(hidden, second_w, preferred_element_type=jnp.float32)
    normed, inv_scale = layer_norm(output)
    return (pre_act, normed, inv_scale)


def mlp_backward(upstream, pre_act, normed, inv_scale, first_w, second_w):
    grad_out = norm_backward(upstream, normed, inv_scale).astype(jnp.bfloat16)
    grad_hidden = jnp.dot(grad_out, second_w.T, preferred_element_type=jnp.float32)
    grad_pre = (grad_hidden * swish_slope(pre_act)).astype(jnp.bfloat16)
    return jnp.dot(grad_pre, first_w.T, preferred_element_type=jnp.float32)


def node_backward(node_feat, aggregate, upstream_bf, node_w1, node_w2):
    feat_width = node_feat.shape[1]
    inputs_cat = jnp.concatenate([node_feat, aggregate.astype(jnp.bfloat16)], 1)
    pre_act, normed, inv_scale = mlp_forward(inputs_cat, node_w1, node_w2)
    upstream = upstream_bf.astype(jnp.float32)
    grad_in = mlp_backward(upstream, pre_act, normed, inv_scale, node_w1, node_w2)
    return (upstream + grad_in[:, :feat_width], grad_in[:, feat_width:])


def select_cols(indices, offset, span_rows, dtype):
    columns = jnp.arange(span_rows, dtype=jnp.int32)[None, :]
    return (indices[:, None] - offset == columns).astype(dtype)


def fold_bf16(indices, shard_rows, offset):
    picker = select_cols(indices, offset, shard_rows.shape[0], jnp.bfloat16)
    return jnp.dot(picker, shard_rows, preferred_element_type=jnp.float32)


def scatter_term(indices, values, offset, span_rows):
    picker = select_cols(indices, offset, span_rows, jnp.float32)
    return jnp.dot(picker.T, values, precision=lax.Precision.HIGHEST)


def local(
    nodes,
    edges,
    send_local,
    recv_local,
    edge_count,
    edge_w1,
    edge_w2,
    node_w1,
    node_w2,
    grad_nodes_out,
    grad_edges_out,
):
    node_rows = nodes.shape[0]
    edge_slots = edges.shape[2]
    feat_width = edges.shape[3]
    edge_feat = edges[0, 0]
    send_idx = send_local[0, 0]
    recv_idx = recv_local[0, 0]
    live_mask = (jnp.arange(edge_slots, dtype=jnp.int32) < edge_count[0, 0]).astype(jnp.float32)[
        :, None
    ]
    sender_edge = fold_bf16(
        send_idx, lax.all_gather(nodes, "rcv", axis=0, tiled=True), jnp.int32(0)
    ).astype(jnp.bfloat16)
    group_nodes, group_upstream = (
        lax.all_gather(nodes, "snd", axis=0, tiled=True),
        lax.all_gather(grad_nodes_out, "snd", axis=0, tiled=True),
    )
    picker = select_cols(recv_idx, 0, group_nodes.shape[0], jnp.bfloat16)
    receiver_edge = jnp.dot(picker, group_nodes, preferred_element_type=jnp.float32).astype(
        jnp.bfloat16
    )
    inputs_cat = jnp.concatenate([edge_feat, sender_edge, receiver_edge], 1)
    pre_act, normed, inv_scale = mlp_forward(inputs_cat, edge_w1, edge_w2)
    picker_f32 = picker.astype(jnp.float32)
    partial_agg = jnp.dot(picker_f32.T, normed * live_mask, precision=lax.Precision.HIGHEST)
    aggregate = lax.psum(partial_agg.astype(jnp.bfloat16), "snd").astype(jnp.float32)
    direct_all, agg_grad_all = node_backward(
        group_nodes, aggregate, group_upstream, node_w1, node_w2
    )
    direct = lax.dynamic_slice_in_dim(direct_all, lax.axis_index("snd") * node_rows, node_rows, 0)
    agg_grad_edge = jnp.dot(picker_f32, agg_grad_all, precision=lax.Precision.HIGHEST)
    cotangent = grad_edges_out[0, 0].astype(jnp.float32)
    upstream = (cotangent + agg_grad_edge) * live_mask
    grad_in = mlp_backward(upstream, pre_act, normed, inv_scale, edge_w1, edge_w2)
    edge_grad = live_mask * cotangent + grad_in[:, :feat_width]
    send_part = grad_in[:, feat_width : 2 * feat_width]
    recv_part = grad_in[:, 2 * feat_width :]
    send_own = lax.psum_scatter(
        scatter_term(send_idx, send_part, jnp.int32(0), node_rows * lax.axis_size("rcv")).astype(
            jnp.bfloat16
        ),
        "rcv",
        scatter_dimension=0,
        tiled=True,
    ).astype(jnp.float32)
    recv_own = lax.psum_scatter(
        scatter_term(recv_idx, recv_part, jnp.int32(0), node_rows * lax.axis_size("snd")).astype(
            jnp.bfloat16
        ),
        "snd",
        scatter_dimension=0,
        tiled=True,
    ).astype(jnp.float32)
    return (direct + send_own + recv_own, edge_grad[None, None])


def solution(mesh):
    in_specs = (
        P(("snd", "rcv"), None),
        P("snd", "rcv", None, None),
        P("snd", "rcv", None),
        P("snd", "rcv", None),
        P("snd", "rcv"),
        P(),
        P(),
        P(),
        P(),
        P(("snd", "rcv"), None),
        P("snd", "rcv", None, None),
    )
    out_specs = (P(("snd", "rcv"), None), P("snd", "rcv", None, None))
    return jax.shard_map(local, mesh=mesh, in_specs=in_specs, out_specs=out_specs, check_vma=False)
```

profile of v0, /device:TPU:2, one launch (start us, length us, event | category | flops | bytes accessed | tf_op | source)
XLA Modules:
  0.0 394.0 jit_solution(5266284681063897507)
XLA Ops:
  7.2 0.0 copy-start
  7.2 0.0 all-reduce.2.cloned.1.call-start
  7.2 36.5 %all_gather.11 = bf16[128,512]{1,0:T(8,128)(2,1)S(1)} all-gather(bf16[8,512]{1,0:T(8,128)(2,1)} %param.11), channel_id=1, replica_groups=mesh['snd'=32,'rcv'=16] {'rcv'}, dimensions={0}, use_global_device_ids=true | all-gather | bytes 139264 | tf_op jit(solution)/shard_map/all_gather | solution.py:88
  43.7 24.8 %all_gather.10 = bf16[256,512]{1,0:T(8,128)(2,1)S(1)} all-gather(bf16[8,512]{1,0:T(8,128)(2,1)} %param.11), channel_id=1, replica_groups=mesh['snd'=32,'rcv'=16] {'snd'}, dimensions={0}, use_global_device_ids=true | all-gather | bytes 270336 | tf_op jit(solution)/shard_map/all_gather | solution.py:91
  69.1 0.9 convolution_convert_fusion.3
  70.1 1.0 convolution_convert_fusion.2
  71.0 0.0 copy-done
  71.0 0.0 copy-start.5
  71.1 1.6 fusion.5
  72.6 0.0 copy-done.5
  72.6 0.0 copy-start.7
  72.7 0.0 copy-start.2
  72.7 0.0 copy-start.3
  72.7 0.4 fusion.69
  73.1 0.2 multiply_reduce_fusion.3
  73.3 0.1 copy-done.7
  73.5 0.0 copy-done.2
  73.5 1.3 convolution_convert_fusion.1
  74.8 0.0 all-reduce.2.cloned.1.call-update
  74.8 0.0 reduce-scatter.3.cloned.1.call-start
  74.8 0.0 copy-done.3
  74.8 23.1 %all_gather.9 = bf16[256,512]{1,0:T(8,128)(2,1)S(1)} all-gather(bf16[8,512]{1,0:T(8,128)(2,1)S(1)} %copy-done.3), channel_id=1, replica_groups=mesh['snd'=32,'rcv'=16] {'snd'}, dimensions={0}, use_global_device_ids=true | all-gather | bytes 270336 | tf_op jit(solution)/shard_map/all_gather | solution.py:92
  97.9 102.9 %all-reduce.2.cloned.1.call-done = bf16[256,512]{1,0:T(8,128)(2,1)} async-done(((bf16[256,512]{1,0:T(8,128)(2,1)}), bf16[256,512]{1,0:T(8,128)(2,1)}) %all-reduce.2.cloned.1.call-update) | async-done | bytes 262160 | tf_op jit(solution)/shard_map/psum | solution.py:102
  200.8 1.7 fusion.16
  202.6 0.0 copy-start.6
  202.6 1.6 fusion.70
  204.3 0.2 multiply_reduce_fusion.2
  204.5 0.0 copy-done.6
  204.5 0.2 convert_reduce_fusion
  204.8 0.0 copy-start.1
  204.8 3.4 fusion.4
  208.1 0.0 copy-done.1
  208.1 1.7 fusion.68
  209.9 0.0 copy-start.4
  209.9 3.3 fusion.3
  213.2 0.0 copy-done.4
  213.2 2.1 convolution_convert_fusion.4
  215.2 0.0 reduce-scatter.3.cloned.1.call-update
  215.3 0.0 reduce-scatter.5.cloned.1.call-start
  215.3 2.3 convolution_convert_fusion
  217.6 0.0 reduce-scatter.5.cloned.1.call-update
  217.6 0.0 slice-start
  217.6 0.1 convert_element_type.62
  217.7 2.0 fusion.12
  219.7 64.6 %reduce-scatter.3.cloned.1.call-done = bf16[8,512]{1,0:T(8,128)(2,1)} async-done(((bf16[128,512]{1,0:T(8,128)(2,1)}), bf16[8,512]{1,0:T(8,128)(2,1)}) %reduce-scatter.3.cloned.1.call-update) | async-done | bytes 8208 | tf_op jit(solution)/shard_map/reduce_scatter | solution.py:114
  284.2 102.0 %reduce-scatter.5.cloned.1.call-done = bf16[8,512]{1,0:T(8,128)(2,1)} async-done(((bf16[256,512]{1,0:T(8,128)(2,1)}), bf16[8,512]{1,0:T(8,128)(2,1)}) %reduce-scatter.5.cloned.1.call-update) | async-done | bytes 8208 | tf_op jit(solution)/shard_map/reduce_scatter | solution.py:122
  386.2 0.0 slice-done
  386.2 1.3 fusion.61
  (8 shorter events, 0.0 us)
Async XLA Ops:
  7.2 63.9 %copy-start = (bf16[1536,512]{1,0:T(8,128)(2,1)S(1)}, bf16[1536,512]{1,0:T(8,128)(2,1)}, u32[]{:S(2)}) copy-start(bf16[1536,512]{1,0:T(8,128)(2,1)} %param.16) | copy-start | bytes 4718596
  7.2 193.7 %all-reduce.2.cloned.1.call-start = ((), (), s32[]{:S(2)}) async-start(), calls=%async_computation.2 | async-start | bytes 524288 | tf_op jit(solution)/shard_map/psum | solution.py:102
  71.0 1.6 copy-start.5
  72.6 0.8 copy-start.7
  72.7 0.8 copy-start.2
  72.7 2.2 copy-start.3
  74.8 209.4 %reduce-scatter.3.cloned.1.call-start = ((), (), s32[]{:S(2)}) async-start(), calls=%async_computation.3 | async-start | bytes 139264 | tf_op jit(solution)/shard_map/reduce_scatter | solution.py:114
  202.6 1.9 copy-start.6
  204.8 3.4 copy-start.1
  209.9 3.3 copy-start.4
  215.3 170.9 %reduce-scatter.5.cloned.1.call-start = ((), (), s32[]{:S(2)}) async-start(), calls=%async_computation.4 | async-start | bytes 270336 | tf_op jit(solution)/shard_map/reduce_scatter | solution.py:122
  217.6 168.6 %slice-start = ((f32[256,1024]{1,0:T(8,128)}), f32[256,512]{1,0:T(8,128)S(1)}, s32[]{:S(2)}) async-start(f32[256,1024]{1,0:T(8,128)} %fusion.4), calls=%async_computation.5 | async-start | bytes 1048576 | tf_op jit(solution)/shard_map/slice | solution.py:47
Sparse Core Ops, SparseCore 0:
  74.9 125.8 all-reduce.1
  215.4 68.7 reduce-scatter.2
  288.5 97.5 reduce-scatter.4
where the time goes:
time: 395 us; the launch traced here: 394 us
  waiting for transfers between devices  269 us (68%)
  blocking collectives  84.3 us (21%)
  matrix products  21.2 us (5%)
  between operations  14.6 us (4%)
  other arithmetic  4.08 us (1%)
    psum x1, waiting for transfers between devices, local(): lax.psum(partial_agg.astype(jnp.bfloat16), 'snd').astype(jnp.float32)  103 us
    reduce_scatter x1, waiting for transfers between devices, local(): lax.psum_scatter(scatter_term(recv_idx, recv_part, jnp.int32(0), node_row...  102 us
    reduce_scatter x1, waiting for transfers between devices, local(): lax.psum_scatter(scatter_term(send_idx, send_part, jnp.int32(0), node_row...  64.6 us
    all_gather x1, blocking collectives, local(): lax.all_gather(nodes, 'rcv', axis=0, tiled=True)  36.5 us
    all_gather x1, blocking collectives, local(): lax.all_gather(nodes, 'snd', axis=0, tiled=True)  24.8 us
    all_gather x1, blocking collectives, local(): lax.all_gather(grad_nodes_out, 'snd', axis=0, tiled=True)  23.1 us
  transfers between devices with their start and end apart: 3, of which 3 were waited for; matrix products, arithmetic and copies ran while one was open for 1% of the time, Pallas kernels for 0%

commit v1 on v0

--- a/solution.py
+++ b/solution.py
@@ -2,6 +2,11 @@
 import jax.numpy as jnp
 from jax import lax
 from jax.sharding import PartitionSpec as P
+from jax.lax import all_gather
+
+
+def settle_pairs_all_now(sample):
+    return all_gather(sample, "snd").sum(axis=0)
 
 
 def swish_slope(pre_act):
@@ -99,7 +104,7 @@
     pre_act, normed, inv_scale = mlp_forward(inputs_cat, edge_w1, edge_w2)
     picker_f32 = picker.astype(jnp.float32)
     partial_agg = jnp.dot(picker_f32.T, normed * live_mask, precision=lax.Precision.HIGHEST)
-    aggregate = lax.psum(partial_agg.astype(jnp.bfloat16), "snd").astype(jnp.float32)
+    aggregate = settle_pairs_all_now(partial_agg.astype(jnp.bfloat16)).astype(jnp.float32)
     direct_all, agg_grad_all = node_backward(
         group_nodes, aggregate, group_upstream, node_w1, node_w2
     )

time: 395 us -> 335 us (0.85)
  waiting for transfers between devices: 269 us -> 206 us
  other arithmetic: 4.08 us -> 8.84 us
    psum x1 -> x0, waiting for transfers between devices: 103 us -> none  [local(): lax.psum(partial_agg.astype(jnp.bfloat16), 'snd').astype(jnp.float32)]
    all_gather x0 -> x1, waiting for transfers between devices: none -> 39.5 us  [settle_pairs_all_now(): return all_gather(sample, 'snd').sum(axis=0)]
    reduce_sum x0 -> x1, other arithmetic: none -> 4.75 us  [settle_pairs_all_now(): return all_gather(sample, 'snd').sum(axis=0)]
where the time goes in v1:
time: 335 us; the launch traced here: 334 us
  waiting for transfers between devices  206 us (61%)
  blocking collectives  84.4 us (25%)
  matrix products  20 us (6%)
  between operations  14.6 us (4%)
  other arithmetic  8.84 us (3%)
    reduce_scatter x1, waiting for transfers between devices, local(): lax.psum_scatter(scatter_term(recv_idx, recv_part, jnp.int32(0), node_row...  102 us
    reduce_scatter x1, waiting for transfers between devices, local(): lax.psum_scatter(scatter_term(send_idx, send_part, jnp.int32(0), node_row...  64 us
    all_gather x1, waiting for transfers between devices, settle_pairs_all_now(): return all_gather(sample, 'snd').sum(axis=0)  39.5 us
    all_gather x1, blocking collectives, local(): lax.all_gather(nodes, 'rcv', axis=0, tiled=True)  33.5 us
    all_gather x1, blocking collectives, local(): lax.all_gather(nodes, 'snd', axis=0, tiled=True)  27.8 us
    all_gather x1, blocking collectives, local(): lax.all_gather(grad_nodes_out, 'snd', axis=0, tiled=True)  23.1 us
  transfers between devices with their start and end apart: 3, of which 3 were waited for; matrix products, arithmetic and copies ran while one was open for 1% of the time, Pallas kernels for 0%

profile of v1, /device:TPU:2, one launch (start us, length us, event | category | flops | bytes accessed | tf_op | source)
XLA Modules:
  0.0 334.1 jit_solution(927026904238378874)
XLA Ops:
  7.2 0.0 copy-start
  7.2 0.0 all-gather.3.cloned.1.call-start
  7.2 27.8 %all_gather.16 = bf16[256,512]{1,0:T(8,128)(2,1)S(1)} all-gather(bf16[8,512]{1,0:T(8,128)(2,1)} %param.11), channel_id=1, replica_groups=mesh['snd'=32,'rcv'=16] {'snd'}, dimensions={0}, use_global_device_ids=true | all-gather | bytes 270336 | tf_op jit(solution)/shard_map/all_gather | solution.py:96
  35.0 33.5 %all_gather.17 = bf16[128,512]{1,0:T(8,128)(2,1)S(1)} all-gather(bf16[8,512]{1,0:T(8,128)(2,1)} %param.11), channel_id=1, replica_groups=mesh['snd'=32,'rcv'=16] {'rcv'}, dimensions={0}, use_global_device_ids=true | all-gather | bytes 139264 | tf_op jit(solution)/shard_map/all_gather | solution.py:93
  68.5 0.9 convolution_convert_fusion.2
  69.4 0.9 convolution_convert_fusion.3
  70.4 0.0 copy-done
  70.4 0.0 copy-start.6
  70.4 1.6 fusion.5
  72.0 0.0 copy-done.6
  72.0 0.0 copy-start.8
  72.0 0.0 copy-start.2
  72.0 0.0 copy-start.3
  72.0 0.4 fusion.69
  72.5 0.2 multiply_reduce_fusion.3
  72.7 0.2 copy-done.8
  73.5 0.0 copy-done.2
  73.5 1.3 convolution_convert_fusion.1
  74.8 0.0 all-gather.3.cloned.1.call-update
  74.8 0.0 reduce-scatter.3.cloned.1.call-start
  74.9 0.0 copy-done.3
  74.9 23.1 %all_gather.15 = bf16[256,512]{1,0:T(8,128)(2,1)S(1)} all-gather(bf16[8,512]{1,0:T(8,128)(2,1)S(1)} %copy-done.3), channel_id=1, replica_groups=mesh['snd'=32,'rcv'=16] {'snd'}, dimensions={0}, use_global_device_ids=true | all-gather | bytes 270336 | tf_op jit(solution)/shard_map/all_gather | solution.py:97
  98.0 39.5 %all-gather.3.cloned.1.call-done = bf16[8192,512]{1,0:T(8,128)(2,1)} async-done(((bf16[256,512]{1,0:T(8,128)(2,1)}), bf16[8192,512]{1,0:T(8,128)(2,1)}) %all-gather.3.cloned.1.call-update) | async-done | bytes 8388624 | tf_op jit(solution)/shard_map/all_gather | solution.py:9
  137.5 4.8 %reduce_sum.86 = bf16[256,512]{1,0:T(8,128)(2,1)S(1)} reduce(bf16[32,256,512]{2,1,0:T(8,128)(2,1)} %bitcast.22, bf16[]{:T(256)} %constant.27.clone.1), dimensions={0}, to_apply=%region_2.3 | reduce | flops 4063232 | bytes 8650754 | tf_op jit(solution)/shard_map/reduce_sum | solution.py:9
  142.2 0.0 copy-start.5
  142.3 1.7 fusion.16
  144.0 0.0 copy-done.5
  144.0 0.0 copy-start.7
  144.0 0.4 fusion.70
  144.4 0.2 multiply_reduce_fusion.2
  144.6 0.2 copy-done.7
  144.8 0.3 convert_reduce_fusion
  145.1 0.0 copy-start.1
  145.1 3.4 %fusion.4 = f32[256,1024]{1,0:T(8,128)} fusion(bf16[1024,512]{1,0:T(8,128)(2,1)} %param.18, bf16[512,512]{1,0:T(8,128)(2,1)} %param.19, f32[256,512]{1,0:T(8,128)} %copy-done.7, f32[256,512]{1,0:T(8,128)S(1)} %get-tuple-element.9, bf16[256,512]{1,0:T(8,128)(2,1)S(1)} %all_gather.15, f32[256]{0:T(256)S(1)} %get-tuple-element.11, ...), kind=kOutput, calls=%fused_computation.11 | convolution fusion | flops 404881408 | bytes 3936256 | tf_op jit(solution)/shard_map/dot_general | solution.py:43
  148.4 0.0 copy-done.1
  148.4 1.7 fusion.68
  150.1 0.0 copy-start.4
  150.2 3.3 fusion.3
  153.5 0.0 copy-done.4
  153.5 2.1 convolution_convert_fusion.4
  155.5 0.0 reduce-scatter.3.cloned.1.call-update
  155.6 0.0 reduce-scatter.5.cloned.1.call-start
  155.6 2.3 convolution_convert_fusion
  157.9 0.0 reduce-scatter.5.cloned.1.call-update
  157.9 0.0 slice-start
  157.9 0.1 convert_element_type.64
  158.0 2.0 fusion.12
  160.0 64.0 %reduce-scatter.3.cloned.1.call-done = bf16[8,512]{1,0:T(8,128)(2,1)} async-done(((bf16[128,512]{1,0:T(8,128)(2,1)}), bf16[8,512]{1,0:T(8,128)(2,1)}) %reduce-scatter.3.cloned.1.call-update) | async-done | bytes 8208 | tf_op jit(solution)/shard_map/reduce_scatter | solution.py:119
  223.9 102.3 %reduce-scatter.5.cloned.1.call-done = bf16[8,512]{1,0:T(8,128)(2,1)} async-done(((bf16[256,512]{1,0:T(8,128)(2,1)}), bf16[8,512]{1,0:T(8,128)(2,1)}) %reduce-scatter.5.cloned.1.call-update) | async-done | bytes 8208 | tf_op jit(solution)/shard_map/reduce_scatter | solution.py:127
  326.3 0.0 slice-done
  326.3 1.3 fusion.61
  (8 shorter events, 0.0 us)
Async XLA Ops:
  7.2 63.2 %copy-start = (bf16[1536,512]{1,0:T(8,128)(2,1)S(1)}, bf16[1536,512]{1,0:T(8,128)(2,1)}, u32[]{:S(2)}) copy-start(bf16[1536,512]{1,0:T(8,128)(2,1)} %param.16) | copy-start | bytes 4718596
  7.2 130.3 %all-gather.3.cloned.1.call-start = ((), (), s32[]{:S(2)}) async-start(), calls=%async_computation.4 | async-start | bytes 8650752 | tf_op jit(solution)/shard_map/all_gather | solution.py:9
  70.4 1.6 copy-start.6
  72.0 0.8 copy-start.8
  72.0 1.5 copy-start.2
  72.0 2.9 copy-start.3
  74.8 149.1 %reduce-scatter.3.cloned.1.call-start = ((), (), s32[]{:S(2)}) async-start(), calls=%async_computation.2 | async-start | bytes 139264 | tf_op jit(solution)/shard_map/reduce_scatter | solution.py:119
  142.2 1.7 copy-start.5
  144.0 0.8 copy-start.7
  145.1 3.4 %copy-start.1 = (bf16[1,1,256,512]{3,2,1,0:T(8,128)(2,1)S(1)}, bf16[1,1,256,512]{3,2,1,0:T(8,128)(2,1)}, u32[]{:S(2)}) copy-start(bf16[1,1,256,512]{3,2,1,0:T(8,128)(2,1)} %param.21) | copy-start | bytes 786436
  150.1 3.3 copy-start.4
  155.6 170.7 %reduce-scatter.5.cloned.1.call-start = ((), (), s32[]{:S(2)}) async-start(), calls=%async_computation.3 | async-start | bytes 270336 | tf_op jit(solution)/shard_map/reduce_scatter | solution.py:127
  157.9 168.4 %slice-start = ((f32[256,1024]{1,0:T(8,128)}), f32[256,512]{1,0:T(8,128)S(1)}, s32[]{:S(2)}) async-start(f32[256,1024]{1,0:T(8,128)} %fusion.4), calls=%async_computation.5 | async-start | bytes 1048576 | tf_op jit(solution)/shard_map/slice | solution.py:52
Sparse Core Ops, SparseCore 0:
  75.0 62.4 all-gather.2
  155.7 68.2 reduce-scatter.2
  228.9 97.3 reduce-scatter.4
